TPU v7x, 128 devices: a whole 4x4x4 slice. The times are simulated.
128 devices in a mesh: dp: 8 (over y, z_hi), pipe: 2 (over z_lo), ts: 8 (over x, core).
Axes of the slice: x: 4, y: 4, z: 4 (z_hi: 2, z_lo: 2; z = z_hi * 2 + z_lo), core: 2. Of those that a mesh axis runs over, the one named last changes fastest.
Arguments:
- section_inputs: bfloat16 [8, 2, 1, 512, 4096], P('dp', 'pipe', None, 'ts'), may hold values from -6 to 6
- grad_out: bfloat16 [8, 1, 512, 4096], P('dp', None, 'ts'), may hold values from -6 to 6
- in_weight: bfloat16 [2, 4096, 6144], P('pipe', None, 'ts'), may hold values from -0.09375 to 0.09375
- out_weight: bfloat16 [2, 4096, 4096], P('pipe', 'ts'), may hold values from -0.09375 to 0.09375
- gains: bfloat16 [2, 4096], P('pipe'), may hold values from 0.5 to 1.5
- step_weight: bfloat16 [4096, 32], P(None, 'ts'), may hold values from -0.09375 to 0.09375
- decay_rate: float32 [32], P('ts'), may hold values from 0.01 to 1
Outputs:
- input_grads: bfloat16 [8, 2, 1, 512, 4096], P('dp', 'pipe', None, 'ts')
- in_weight_grad: float32 [2, 4096, 6144], P('pipe', 'dp', 'ts')
- out_weight_grad: float32 [2, 4096, 4096], P('pipe', 'ts', 'dp')
- gain_grad: float32 [2, 4096], P('pipe', ('dp', 'ts'))
- step_grad: float32 [4096, 32], P(('dp', 'pipe'), 'ts')
- rate_grad: float32 [32], P('ts')
All inputs are finite; a program needn't handle non-finite values.
Results may differ from a plain program's by a relative error of at most 0.03.
Values may be sent and summed in bfloat16 or wider, within the bound.
A program may use at most 192 MiB of HBM per device.

v0:
```python
import jax
import jax.numpy as jnp
from jax import lax
from jax.sharding import PartitionSpec as P

highest = lax.Precision.HIGHEST
contract_rows = (((0,), (0,)), ((), ()))
contract_cols = (((1,), (1,)), ((), ()))


def from_behind(value, axis, by):
    count = lax.axis_size(axis)
    pairs = [(i, i + by) for i in range(count) if 0 <= i + by < count]
    return lax.ppermute(value, axis, pairs)


def normed(features, scales):
    return (
        features * lax.rsqrt(jnp.mean(features * features, axis=-1, keepdims=True) + 1e-05) * scales
    )


def attend(projected, logits, decay_rates):
    length = projected.shape[0]
    head_count = decay_rates.shape[0]
    head_width = projected.shape[1] // (head_count + 2)
    queries = projected[:, : head_count * head_width].reshape(length, head_count, head_width)
    keys_part = projected[:, head_count * head_width : (head_count + 1) * head_width]
    values_part = projected[:, (head_count + 1) * head_width :]
    scores = jnp.einsum("shd,td->hst", queries, keys_part, precision=highest) * head_width ** (-0.5)
    causal = jnp.arange(length)[:, None] >= jnp.arange(length)[None, :]
    scores = jnp.where(causal[None], scores, -1e30)
    weights = jax.nn.softmax(scores, axis=-1)
    mixed_out = jnp.einsum("hst,td->shd", weights, values_part, precision=highest)
    return mixed_out.reshape(length, head_count * head_width)


def selective(projected, logits, decay_rates):
    length = projected.shape[0]
    head_count = decay_rates.shape[0]
    head_width = projected.shape[1] // (head_count + 2)
    inputs_part = projected[:, : head_count * head_width].reshape(length, head_count, head_width)
    write_part = projected[:, head_count * head_width : (head_count + 1) * head_width]
    read_part = projected[:, (head_count + 1) * head_width :]
    step_sizes = jax.nn.softplus(logits)
    totals = jnp.cumsum(-step_sizes * decay_rates[None, :], axis=0)
    causal = jnp.arange(length)[:, None] >= jnp.arange(length)[None, :]
    log_gaps = jnp.where(causal[:, :, None], totals[:, None, :] - totals[None, :, :], -1e30)
    decays = jnp.exp(log_gaps)
    intersection = jnp.dot(read_part, write_part.T, precision=highest) * head_width ** (-0.5)
    mixing = decays * intersection[:, :, None] * step_sizes[None, :, :]
    mixed_out = jnp.einsum("sth,thd->shd", mixing, inputs_part, precision=highest)
    return mixed_out.reshape(length, head_count * head_width)


def shards(section_inputs, grad_out, in_weight, out_weight, gains, step_weight, decay_rate):
    section_index = lax.axis_index("pipe")
    is_later = section_index == 1
    local_inputs = section_inputs[0, 0]
    cotangents = grad_out[0]
    in_w = in_weight[0]
    out_w = out_weight[0]
    gain_wide = gains[0].astype(jnp.float32)
    micro_count = local_inputs.shape[0]
    row_count = local_inputs.shape[1]
    model_width = local_inputs.shape[2]
    block_width = in_w.shape[1]
    mix_width = out_w.shape[0]
    inputs_wide = local_inputs.astype(jnp.float32)
    normal_local = normed(inputs_wide, gain_wide).astype(jnp.bfloat16)

    def mixer_fn(proj_wide, logit_wide, rate_wide):
        return lax.cond(section_index == 0, attend, selective, proj_wide, logit_wide, rate_wide)

    def local_work(normal_all, upstream):
        projected = jnp.dot(normal_all, in_w, preferred_element_type=jnp.float32).astype(
            jnp.bfloat16
        )
        logits = jnp.dot(normal_all, step_weight, preferred_element_type=jnp.float32)
        mixed_wide, backward = jax.vjp(mixer_fn, projected.astype(jnp.float32), logits, decay_rate)
        mixed = mixed_wide.astype(jnp.bfloat16)
        mix_grad = lax.dot_general(
            upstream, out_w, contract_cols, preferred_element_type=jnp.float32
        ).astype(jnp.bfloat16)
        proj_grad_wide, logit_grad, rates_grad = backward(mix_grad.astype(jnp.float32))
        proj_grad = proj_grad_wide.astype(jnp.bfloat16)
        terms = lax.dot_general(proj_grad, in_w, contract_cols, preferred_element_type=jnp.float32)
        terms = terms + lax.dot_general(
            logit_grad, step_weight.astype(jnp.float32), contract_cols, precision=highest
        )
        return (mixed, proj_grad, terms, logit_grad, rates_grad)

    def skipped_work(normal_all, upstream):
        whole_rows = normal_all.shape[0]
        return (
            jnp.zeros((whole_rows, mix_width), jnp.bfloat16),
            jnp.zeros((whole_rows, block_width), jnp.bfloat16),
            jnp.zeros((whole_rows, model_width), jnp.float32),
            jnp.zeros((whole_rows, step_weight.shape[1]), jnp.float32),
            jnp.zeros(decay_rate.shape, jnp.float32),
        )

    received = jnp.zeros((row_count, model_width), jnp.bfloat16)
    gain_acc = jnp.zeros((model_width,), jnp.float32)
    step_acc = jnp.zeros(step_weight.shape, jnp.float32)
    rate_acc = jnp.zeros(decay_rate.shape, jnp.float32)
    grad_list, normal_list, upstream_list, proj_list, mixed_list = ([], [], [], [], [])
    for step_count in range(micro_count + 1):
        micro_index = step_count - 1 + section_index
        chosen = jnp.clip(micro_index, 0, micro_count - 1)
        valid_flag = (micro_index >= 0) & (micro_index < micro_count)
        is_valid = valid_flag.astype(jnp.float32)
        incoming = jnp.where(is_later, cotangents[min(step_count, micro_count - 1)], received)
        normal_here = lax.dynamic_index_in_dim(normal_local, chosen, 0, keepdims=False)
        normal_all, upstream = (
            lax.all_gather(normal_here, "ts", axis=0, tiled=True),
            lax.all_gather(incoming, "ts", axis=0, tiled=True),
        )
        mixed, proj_grad, terms, logit_grad, rates_grad = lax.cond(
            valid_flag, local_work, skipped_work, normal_all, upstream
        )
        normal_grad = lax.psum_scatter(
            terms.astype(jnp.bfloat16), "ts", scatter_dimension=0, tiled=True
        ).astype(jnp.float32)
        current = lax.dynamic_index_in_dim(inputs_wide, chosen, 0, keepdims=False)
        unused_out, norm_back = jax.vjp(normed, current, gain_wide)
        input_grad, gain_term = norm_back(normal_grad)
        section_grad = (incoming.astype(jnp.float32) + input_grad).astype(jnp.bfloat16)
        gain_acc = gain_acc + is_valid * gain_term
        rate_acc = rate_acc + is_valid * rates_grad
        step_acc = step_acc + is_valid * lax.dot_general(
            normal_all.astype(jnp.float32), logit_grad, contract_rows, precision=highest
        )
        if step_count < micro_count:
            received = from_behind(section_grad, "pipe", -1)
        grad_list.append(section_grad)
        normal_list.append(normal_all)
        upstream_list.append(upstream)
        proj_list.append(proj_grad)
        mixed_list.append(mixed)
    first_step = 1 - section_index

    def valid_steps(collected):
        return lax.dynamic_slice_in_dim(jnp.stack(collected), first_step, micro_count, 0)

    grads_out = valid_steps(grad_list).reshape(1, 1, micro_count, row_count, model_width)
    normal_rows = valid_steps(normal_list).reshape(-1, model_width)
    upstream_rows = valid_steps(upstream_list).reshape(-1, model_width)
    proj_rows = valid_steps(proj_list).reshape(-1, block_width)
    mixed_rows = valid_steps(mixed_list).reshape(-1, mixed_list[0].shape[1])
    first_part = lax.dot_general(
        normal_rows, proj_rows, contract_rows, preferred_element_type=jnp.float32
    )
    second_part = lax.dot_general(
        upstream_rows, mixed_rows, contract_rows, preferred_element_type=jnp.float32
    )
    gradient_sums = lax.psum_scatter(
        jnp.concatenate([first_part, second_part], axis=1).astype(jnp.bfloat16),
        "dp",
        scatter_dimension=0,
        tiled=True,
    ).astype(jnp.float32)
    in_grad = gradient_sums[:, :block_width][None]
    out_grad = gradient_sums[:, block_width:].T[None]
    gain_out = lax.psum_scatter(gain_acc, ("dp", "ts"), scatter_dimension=0, tiled=True)[None]
    step_out = lax.psum_scatter(
        step_acc.astype(jnp.bfloat16), ("dp", "pipe"), scatter_dimension=0, tiled=True
    ).astype(jnp.float32)
    rate_out = lax.psum(rate_acc, ("dp", "pipe"))
    return (grads_out, in_grad, out_grad, gain_out, step_out, rate_out)


def solution(mesh):
    return jax.shard_map(
        shards,
        mesh=mesh,
        in_specs=(
            P("dp", "pipe", None, "ts", None),
            P("dp", None, "ts", None),
            P("pipe", None, "ts"),
            P("pipe", "ts", None),
            P("pipe", None),
            P(None, "ts"),
            P("ts"),
        ),
        out_specs=(
            P("dp", "pipe", None, "ts", None),
            P("pipe", "dp", "ts"),
            P("pipe", "ts", "dp"),
            P("pipe", ("dp", "ts")),
            P(("dp", "pipe"), "ts"),
            P("ts"),
        ),
        check_vma=False,
    )
```

profile of v0, /device:TPU:0, one launch (start us, length us, event | category | flops | bytes accessed | tf_op | source)
XLA Modules:
  0.0 846.9 jit_solution(7184446754458900160)
XLA Ops:
  14.1 30.8 %all-gather.4.cloned.1.call-done = bf16[512,4096]{1,0:T(8,128)(2,1)} async-done(((bf16[64,4096]{1,0:T(8,128)(2,1)}), bf16[512,4096]{1,0:T(8,128)(2,1)}) %all-gather.4.cloned.1.call-update) | async-done | bytes 4194320 | tf_op jit(solution)/shard_map/all_gather | solution.py:117
  44.9 34.4 %all-gather.6.cloned.1.call-done = bf16[512,4096]{1,0:T(8,128)(2,1)} async-done(((bf16[64,4096]{1,0:T(8,128)(2,1)}), bf16[512,4096]{1,0:T(8,128)(2,1)}) %all-gather.6.cloned.1.call-update) | async-done | bytes 4194320 | tf_op jit(solution)/shard_map/all_gather | solution.py:116
  79.2 9.6 %conditional.10 = (bf16[512,4096]{1,0:T(8,128)(2,1)}, f32[512,4]{0,1:T(4,128)}, f32[4]{0:T(128)S(1)}, bf16[1,512,512]{1,2,0:T(8,128)(2,1)}, bf16[1,512,768]{2,1,0:T(8,128)(2,1)}) conditional(s32[]{:T(128)} %convert_element_type.196, () %tuple.105, (s32[]{:T(128)}, bf16[512,4096]{1,0:T(8,128)(2,1)}, bf16[512,4096]{1,0:T(8,128)(2,1)}, ...), branch_computations={%region_1.2_spmd, %region_2.20_spmd} | conditional | flops 18401460224 | bytes 301368480 | solution.py:119
  89.4 119.4 %reduce-scatter.7.cloned.1.call-done = bf16[64,4096]{1,0:T(8,128)(2,1)} async-done(((bf16[512,4096]{1,0:T(8,128)(2,1)}), bf16[64,4096]{1,0:T(8,128)(2,1)}) %reduce-scatter.7.cloned.1.call-update) | async-done | bytes 524304 | tf_op jit(solution)/shard_map/reduce_scatter | solution.py:122
  214.5 11.3 %collective-permute-done = bf16[64,4096]{1,0:T(8,128)(2,1)S(1)} collective-permute-done((bf16[64,4096]{1,0:T(8,128)(2,1)S(1)}, bf16[64,4096]{1,0:T(8,128)(2,1)S(1)}, u32[]{:S(2)}, u32[]{:S(2)}) %collective-permute-start) | collective-permute-done | bytes 524320 | tf_op jit(solution)/shard_map/ppermute | solution.py:14
  230.7 29.2 %all-gather.8.cloned.1.call-done = bf16[512,4096]{1,0:T(8,128)(2,1)} async-done(((bf16[64,4096]{1,0:T(8,128)(2,1)}), bf16[512,4096]{1,0:T(8,128)(2,1)}) %all-gather.8.cloned.1.call-update) | async-done | bytes 4194320 | tf_op jit(solution)/shard_map/all_gather | solution.py:117
  259.9 122.6 %conditional.11 = (bf16[512,4096]{1,0:T(8,128)(2,1)}, f32[512,4]{0,1:T(4,128)}, f32[4]{0:T(128)}, bf16[1,512,512]{1,2,0:T(8,128)(2,1)S(1)}, bf16[1,512,768]{2,1,0:T(8,128)(2,1)}) conditional(s32[]{:T(128)} %convert_element_type.207, () %tuple.107, (s32[]{:T(128)}, bf16[512,4096]{1,0:T(8,128)(2,1)}, bf16[512,4096]{1,0:T(8,128)(2,1)}, ...), branch_computations={%region_22.24_spmd, %region_23.41_spmd} | conditional | flops 18401460224 | bytes 284459808 | solution.py:119
  259.9 7.2 fusion.78
  268.3 49.3 %conditional.6 = (f32[512,4]{0,1:T(4,128)S(1)}, f32[1,4]{1,0:T(1,128)S(1)}, f32[512,4]{0,1:T(4,128)S(1)}, pred[512,512,4]{1,0,2:T(32,128)(4,1)}, f32[512,512,4]{...) conditional(s32[]{:T(128)} %convert_element_type.168, ...), branch_computations={%region_24.27_spmd, %region_27.30_spmd} | conditional | flops 3230138368 | bytes 115712336
  317.6 7.0 fusion.79
  324.6 45.8 %conditional.7 = (f32[512,4]{0,1:T(4,128)}, f32[4]{0:T(128)}, bf16[512,768]{1,0:T(8,128)(2,1)S(1)}, bf16[1,512,768]{2,1,0:T(8,128)(2,1)}) conditional(s32[]{:T(128)} %convert_element_type.168, (f32[512,512]{1,0:T(8,128)}, f32[512,4,128]{0,2,1:T(8,128)S(1)}, f32[512,512,4]{1,0,2:T(8,128)}, f32[1,512,4]{1,2,0:T(4,128)S(1)}, ...), branch_computations={%region_30.38_spmd, %region_38.40_spmd} | conditional | flops 6458441728 | bytes 93954192
  325.0 5.3 copy.150
  333.4 6.9 multiply_reduce_fusion.1
  345.2 6.9 fusion.24
  352.2 5.3 fusion.20
  359.1 8.7 %convolution_bitcast_fusion.1 = f32[512,128]{1,0:T(8,128)S(1)} fusion(f32[4,512,512]{2,1,0:T(8,128)} %get-tuple-element.602, f32[128,4,512]{2,0,1:T(8,128)S(1)} %bitcast.410), kind=kOutput, calls=%fused_computation.43 | convolution fusion | flops 1610612736 | bytes 5505024 | tf_op jit(solution)/shard_map/cond/branch_1_fun/transpose(jvp())/cond/branch_1_fun/hst,td->shd/dot_general | solution.py:34
  370.4 5.6 fusion.136
  376.0 6.3 convolution_add_fusion.1
  393.6 5.5 convolution_convert_fusion.8
  399.0 9.8 %pad_maximum_fusion = bf16[4096,1280]{0,1:T(8,128)(2,1)} fusion(bf16[4096,512]{0,1:T(8,128)(2,1)S(1)} %convolution_convert_fusion.9, bf16[4096,768]{0,1:T(8,128)(2,1)S(1)} %convolution_convert_fusion.8), kind=kLoop, calls=%fused_computation.154 | loop fusion | flops 20971520 | bytes 20971520 | tf_op jit(solution)/shard_map/concatenate | solution.py:158
  411.4 36.6 %psum.7 = f32[4]{0:T(128)} all-reduce(f32[4]{0:T(128)S(1)} %multiply_add_fusion.1), channel_id=1, replica_groups=mesh['dp'=8,'pipe'=2,'ts'=8] {'dp','pipe'}, use_global_device_ids=true, to_apply=%region_47.49 | all-reduce | flops 4 | bytes 32 | tf_op jit(solution)/shard_map/psum | solution.py:169
  448.0 13.1 %reduce-scatter.13.cloned.1.call-done = bf16[256,4]{1,0:T(8,128)(2,1)} async-done(((bf16[4096,4]{1,0:T(8,128)(2,1)}), bf16[256,4]{1,0:T(8,128)(2,1)}) %reduce-scatter.13.cloned.1.call-update) | async-done | bytes 2064
  462.7 37.9 %reduce-scatter.9.cloned.1.call-done = bf16[64,4096]{1,0:T(8,128)(2,1)} async-done(((bf16[512,4096]{1,0:T(8,128)(2,1)}), bf16[64,4096]{1,0:T(8,128)(2,1)}) %reduce-scatter.9.cloned.1.call-update) | async-done | bytes 524304 | tf_op jit(solution)/shard_map/reduce_scatter | solution.py:122
  502.1 330.3 %all-reduce.12 = f32[4096]{0:T(1024)S(1)} all-reduce(f32[4096]{0:T(1024)S(1)} %multiply_add_fusion), channel_id=5, replica_groups=mesh['dp'=8,'pipe'=2,'ts'=8] {'dp','ts'}, use_global_device_ids=true, to_apply=%region_45.47.clone | all-reduce | flops 4096 | bytes 32768
  (139 shorter events, 99.4 us)
Async XLA Ops:
  7.2 37.7 %all-gather.4.cloned.1.call-start = ((), (), s32[]{:S(2)}) async-start(), calls=%async_computation.4 | async-start | bytes 4718592 | tf_op jit(solution)/shard_map/all_gather | solution.py:117
  7.9 71.4 %copy-start.43 = (f32[4]{0:T(128)}, f32[4]{0:T(128)S(1)}, u32[]{:S(2)}) copy-start(f32[4]{0:T(128)S(1)} %copy.316) | copy-start | bytes 52
  9.8 69.5 %all-gather.6.cloned.1.call-start = ((), (), s32[]{:S(2)}) async-start(), calls=%async_computation.5 | async-start | bytes 4718592 | tf_op jit(solution)/shard_map/all_gather | solution.py:116
  14.0 194.8 %reduce-scatter.7.cloned.1.call-start = ((), (), s32[]{:S(2)}) async-start(), calls=%async_computation.6 | async-start | bytes 4718592 | tf_op jit(solution)/shard_map/reduce_scatter | solution.py:122
  88.9 119.9 %copy-start.7 = (bf16[1,1,1,64,4096]{4,3,2,1,0:T(8,128)(2,1)S(1)}, bf16[1,1,1,64,4096]{4,3,2,1,0:T(8,128)(2,1)}, u32[]{:S(2)}) copy-start(bf16[1,1,1,64,4096]{4,3,2,1,0:T(8,128)(2,1)} %param.20) | copy-start | bytes 1572868
  88.9 122.0 %copy-start.19 = (bf16[1,1,64,4096]{3,2,1,0:T(8,128)(2,1)S(1)}, bf16[1,1,64,4096]{3,2,1,0:T(8,128)(2,1)}, u32[]{:S(2)}) copy-start(bf16[1,1,64,4096]{3,2,1,0:T(8,128)(2,1)} %param.21) | copy-start | bytes 1572868
  88.9 171.0 %all-gather.8.cloned.1.call-start = ((), (), s32[]{:S(2)}) async-start(), calls=%async_computation.7 | async-start | bytes 4718592 | tf_op jit(solution)/shard_map/all_gather | solution.py:117
  89.4 137.3 %copy-start.41 = (f32[64]{0:T(128)}, f32[64]{0:T(128)S(1)}, u32[]{:S(2)}) copy-start(f32[64]{0:T(128)S(1)} %fusion.122) | copy-start | bytes 772
  210.9 49.0 %copy-start.37 = (bf16[4096,4]{0,1:T(4,128)(2,1)S(1)}, bf16[4096,4]{0,1:T(4,128)(2,1)}, u32[]{:S(2)}) copy-start(bf16[4096,4]{0,1:T(4,128)(2,1)} %param.25) | copy-start | bytes 98308
  210.9 49.0 %copy-start.44 = (f32[4]{0:T(128)S(1)}, f32[4]{0:T(128)}, u32[]{:S(2)}) copy-start(f32[4]{0:T(128)} %copy-done.43) | copy-start | bytes 52
  213.2 12.6 %collective-permute-start = (bf16[64,4096]{1,0:T(8,128)(2,1)S(1)}, bf16[64,4096]{1,0:T(8,128)(2,1)S(1)}, u32[]{:S(2)}, u32[]{:S(2)}) collective-permute-start(bf16[64,4096]{1,0:T(8,128)(2,1)S(1)} %fusion.108), channel_id=1, source_target_pairs={{8,0},{9,1},{10,2},{11,3},{12,4},{13,5},{14,6},{15,7},{24,16},{25,... | collective-permute-start | bytes 1572872 | tf_op jit(solution)/shard_map/ppermute | solution.py:14
  226.7 234.5 %reduce-scatter.13.cloned.1.call-start = ((), (), s32[]{:S(2)}) async-start(), calls=%async_computation.10 | async-start | bytes 1114112
  259.9 7.2 copy-start.2
  317.6 7.0 copy-start.39
  345.2 7.0 copy-start.9
  345.2 7.0 copy-start.22
  345.2 7.0 copy-start.35
  376.0 6.3 copy-start.40
  387.9 112.7 %reduce-scatter.9.cloned.1.call-start = ((), (), s32[]{:S(2)}) async-start(), calls=%async_computation.8 | async-start | bytes 4718592 | tf_op jit(solution)/shard_map/reduce_scatter | solution.py:122
  388.4 447.0 %reduce-scatter.11.cloned.1.call-start = ((), (), s32[]{:S(2)}) async-start(), calls=%async_computation.9 | async-start | bytes 11796480 | tf_op jit(solution)/shard_map/reduce_scatter | solution.py:157
  408.9 91.7 %copy-start.42 = (f32[64]{0:T(128)S(1)}, f32[64]{0:T(128)}, u32[]{:S(2)}) copy-start(f32[64]{0:T(128)} %copy-done.41) | copy-start | bytes 772
  408.9 424.1 %copy-start.51 = (f32[64]{0:T(128)S(1)}, f32[64]{0:T(128)}, u32[]{:S(2)}) copy-start(f32[64]{0:T(128)} %get-tuple-element.643) | copy-start | bytes 772
  408.9 424.1 %copy-start.20 = (bf16[64,4096]{1,0:T(8,128)(2,1)S(1)}, bf16[64,4096]{1,0:T(8,128)(2,1)}, u32[]{:S(2)}) copy-start(bf16[64,4096]{1,0:T(8,128)(2,1)} %bitcast_select_fusion.2) | copy-start | bytes 1572868
  408.9 425.5 %copy-start.33 = (bf16[64,4096]{1,0:T(8,128)(2,1)S(1)}, bf16[64,4096]{1,0:T(8,128)(2,1)}, u32[]{:S(2)}) copy-start(bf16[64,4096]{1,0:T(8,128)(2,1)} %copy-done.32) | copy-start | bytes 1572868
  (10 other events, 24.2 us)
Sparse Core Ops, SparseCore 0:
  10.3 34.5 all-gather.3
  47.2 32.0 all-gather.5
  89.1 119.7 reduce-scatter.6
  226.8 33.0 all-gather.7
  388.0 73.1 reduce-scatter.12
  463.5 37.0 reduce-scatter.8
  505.0 133.1 reduce-scatter.10
where the time goes:
time: 856 us; the launch traced here: 847 us
  blocking collectives  367 us (43%)
  waiting for transfers between devices  277 us (32%)
  matrix products  82 us (10%)
  local copies, waits for them, and re-layouts  59.9 us (7%)
  other arithmetic  29.8 us (3%)
  between operations  15.2 us (2%)
  loops' own time  14.7 us (2%)
    unnamed x1, blocking collectives  330 us
    reduce_scatter x2, waiting for transfers between devices, shards(): lax.psum_scatter(terms.astype(jnp.bfloat16), 'ts', scatter_dimension=0, t...  157 us
    all_gather x2, waiting for transfers between devices, shards(): lax.all_gather(incoming, 'ts', axis=0, tiled=True)  60 us
    another operation x42, local copies, waits for them, and re-layouts  43.9 us
    psum x1, blocking collectives, shards(): rate_out = lax.psum(rate_acc, ('dp', 'pipe'))  36.6 us
    all_gather x1, waiting for transfers between devices, shards(): lax.all_gather(normal_here, 'ts', axis=0, tiled=True)  34.4 us
    dot_general x3, matrix products, attend(): jnp.einsum('hst,td->shd', weights, values_part, precision=highest)  19.1 us
    dot_general x3, matrix products, attend(): jnp.einsum('shd,td->hst', queries, keys_part, precision=highest)  17.4 us
  transfers between devices with their start and end apart: 8, of which 7 were waited for; matrix products, arithmetic and copies ran while one was open for 4% of the time, Pallas kernels for 0%

commit v1 on v0

v1 whole, which is shorter than its diff:
```python
import jax
import jax.numpy as jnp
from jax import lax
from jax.experimental import pallas as pl
from jax.experimental.pallas import tpu as pltpu
from jax.sharding import PartitionSpec as P

F32 = jnp.float32
BF16 = jnp.bfloat16
HIGHEST = lax.Precision.HIGHEST
D = 4096
SEQ = 512
HD = 128
HEADS = 4
BW = 768
MW = 512
CH = 4
HS = 16
OWN = 64
AUX = 16
SCALE = HD**-0.5
HALF = D // 2


def mm(a, b, **kw):
    return lax.dot_general(a, b, (((1,), (0,)), ((), ())), preferred_element_type=F32, **kw)


def mm_nt(a, b, **kw):
    return lax.dot_general(a, b, (((1,), (1,)), ((), ())), preferred_element_type=F32, **kw)


def mm_tn(a, b, **kw):
    return lax.dot_general(a, b, (((0,), (0,)), ((), ())), preferred_element_type=F32, **kw)


def aligned(value, by):
    return pl.multiple_of(value, by)


def kernel(
    x_ref, go_hbm, inw_hbm, outw_hbm, gain_ref, step_ref, rate_ref,
    ig_ref, ing_ref, outg_ref, gaing_ref, aux_ref,
    nall, up, inw, outw, proj, projg, mixg, mixed, pbuf, xd, lrow, lcol, dtb, lgb, dl, acc,
    pgc, terms, xsib, rl, rb, nd, dd, ma, pa, sm, gacc, gx, auxr, swt_ref,
    lsem, ssem, rsem,
):
    d = lax.axis_index("dp")
    p = lax.axis_index("pipe")
    t = lax.axis_index("ts")
    x, c = t // 2, t % 2
    y, z = d // 2, d % 2
    xr, xl, x2 = (x + 1) % 4, (x + 3) % 4, (x + 2) % 4
    yu, yd, y2 = (y + 1) % 4, (y + 3) % 4, (y + 2) % 4
    right, left, far, sib = (d, p, xr * 2 + c), (d, p, xl * 2 + c), (d, p, x2 * 2 + c), (d, p, x * 2 + 1 - c)
    other = (d, 1 - p, t)
    upper, lower, zpar = (yu * 2 + z, p, t), (yd * 2 + z, p, t), (y * 2 + 1 - z, p, t)
    yfar = (y2 * 2 + z, p, t)
    peers = {(i, j): (((y + i) % 4) * 2 + (z + j) % 2, p, t) for i in range(4) for j in range(2) if i or j}

    names = {}

    def rc(name, src, dst, dev):
        k = names.setdefault(name, len(names))
        return pltpu.make_async_remote_copy(
            src, dst, ssem.at[k], rsem.at[k], device_id=dev, device_id_type=pl.DeviceIdType.MESH
        )

    def base(xx, cc, off=0):
        return aligned((xx * 2 + cc) * OWN + off, HS)

    cp_in = pltpu.make_async_copy(inw_hbm, inw, lsem.at[0])
    cp_out = pltpu.make_async_copy(outw_hbm, outw, lsem.at[1])
    cp_go = pltpu.make_async_copy(go_hbm, up.at[pl.ds(base(x, c), OWN)], lsem.at[2])
    cp_in.start()
    cp_out.start()

    @pl.when(p == 1)
    def _():
        cp_go.start()

    bar = pltpu.get_barrier_semaphore()
    partners = (right, left, far, sib, other) + tuple(peers.values())
    for dev in partners:
        pl.semaphore_signal(bar, inc=1, device_id=dev, device_id_type=pl.DeviceIdType.MESH)

    xw = x_ref[...].astype(F32)
    gw = gain_ref[...].astype(F32)
    rinv = lax.rsqrt(jnp.mean(xw * xw, axis=-1, keepdims=True) + 1e-05)
    nall[pl.ds(base(x, c), OWN)] = (xw * rinv * gw).astype(BF16)
    pl.semaphore_wait(bar, len(partners))

    def gather(key, buf, off, n, stacked=False):
        def part(xx, half=None, cc=c):
            rows = pl.ds(base(xx, cc, off), n)
            if stacked:
                return buf.at[pl.ds((half or 0) * 4, 8 if half is None else 4), rows]
            if half is None:
                return buf.at[rows]
            return buf.at[rows, pl.ds(half * HALF, HALF)]

        def move(k, ref, dev):
            return rc((key, k), ref, ref, dev)

        g = dict(
            ra=move("ra", part(x, 0), right), lb=move("lb", part(x, 1), left), s=move("s", part(x), sib),
            rb=move("rb", part(x, 1), right), la=move("la", part(x, 0), left),
            fr=move("fr", part(xl, 0), right), fl=move("fl", part(xr, 1), left),
            s1=move("s1", part(xl), sib), s2=move("s2", part(xr), sib), s3=move("s3", part(x2), sib),
        )

        def start():
            for k in ("ra", "lb", "s", "rb", "la"):
                g[k].start()

        def mid():
            g["ra"].wait_recv()
            g["fr"].start()
            g["lb"].wait_recv()
            g["fl"].start()
            g["rb"].wait_recv()
            g["s1"].start()
            g["la"].wait_recv()
            g["s2"].start()

        def end():
            g["fr"].wait_recv()
            g["fl"].wait_recv()
            g["s3"].start()
            for k in ("s", "s1", "s2", "s3"):
                g[k].wait_recv()

        def sent():
            for k in g:
                g[k].wait_send()

        return start, mid, end, sent

    n_start, n_mid, n_end, n_sent = gather("n", nall, 0, OWN)
    n_start()

    def spread(key, buf, dst):
        mine = pl.ds(base(x, c), OWN)
        copies = [
            rc((key, rel), buf.at[mine, pl.ds(aligned(dev[0] * 512, 512), 512)], dst.at[d, mine], dev)
            for rel, dev in peers.items()
        ]

        def start():
            for copy in copies:
                copy.start()
            dst[d, mine] = buf[mine, pl.ds(aligned(d * 512, 512), 512)]

        def arrive():
            for copy in copies:
                copy.wait_recv()

        def sent():
            for copy in copies:
                copy.wait_send()

        return start, arrive, sent

    ns_start, ns_arrive, ns_sent = spread("ns", nall, nd)
    ds_start, ds_arrive, ds_sent = spread("ds", up, dd)
    nx_start, nx_mid, nx_end, nx_sent = gather("nx", nd, 0, OWN, True)
    dx_start, dx_mid, dx_end, dx_sent = gather("dx", dd, 0, OWN, True)
    ns_start()
    swt_ref[...] = jnp.zeros_like(swt_ref)
    swt_ref[0:HEADS] = step_ref[...]
    n_mid()

    @pl.when(p == 1)
    def _():
        u_start, _m, _e, _s = gather("u", up, 0, OWN)
        cp_go.wait()
        u_start()
        ds_start()

    n_end()
    cp_in.wait()

    @pl.loop(0, 2)
    def _(i):
        rows = pl.ds(aligned(i * 256, 256), 256)
        proj[rows] = mm(nall[rows], inw[...]).astype(BF16)

    def causal(tb):
        r = lax.broadcasted_iota(jnp.int32, (HD, SEQ), 0) + tb * HD
        return r >= lax.broadcasted_iota(jnp.int32, (HD, SEQ), 1)

    def hc(h):
        return slice(h * HD, (h + 1) * HD)

    def mix_gradient():
        @pl.loop(0, 2)
        def _(i):
            rows = pl.ds(aligned(i * 256, 256), 256)
            mixg[rows] = mm_nt(up[rows], outw[...]).astype(BF16)

    lane = lax.broadcasted_iota(jnp.int32, (SEQ, HD), 1)

    def rates_row():
        one = lax.broadcasted_iota(jnp.int32, (1, HD), 1)
        row = jnp.zeros((1, HD), F32)
        for h in range(HEADS):
            row = jnp.where(one == h, rate_ref[h], row)
        return row

    def ssm_steps():
        lg = mm_nt(nall[...], swt_ref[...])
        lgb[...] = jnp.zeros_like(lgb)
        lgb[:, 0:AUX] = lg
        lgw = lgb[...]
        dt = jnp.maximum(lgw, 0.0) + jnp.log1p(jnp.exp(-jnp.abs(lgw)))
        dtb[...] = dt
        steps = -dt * rates_row()
        tril = (
            lax.broadcasted_iota(jnp.int32, (SEQ, SEQ), 0) >= lax.broadcasted_iota(jnp.int32, (SEQ, SEQ), 1)
        ).astype(F32)
        totals = mm(tril, steps, precision=HIGHEST)
        lcol[...] = totals
        lrow[...] = totals.T
        for h in range(HEADS):
            xd[:, hc(h)] = (proj[:, hc(h)].astype(F32) * dt[:, h : h + 1]).astype(BF16)

    def ssm_forward():
        @pl.loop(0, 4)
        def _(tb):
            rows = pl.ds(aligned(tb * HD, HD), HD)
            inter = mm_nt(proj[rows, 640:768], proj[:, 512:640]) * SCALE
            mask = causal(tb)
            lc = lcol[rows]
            for h in range(HEADS):
                e = jnp.exp(jnp.where(mask, lc[:, h : h + 1] - lrow[h : h + 1, :], -1e30))
                m = (e * inter).astype(BF16)
                pbuf[h, rows] = m
                mixed[rows, hc(h)] = mm(m, xd[:, hc(h)]).astype(BF16)

    def ssm_backward():
        small_lane = lax.broadcasted_iota(jnp.int32, (HD, HD), 1)

        for tb in range(4):
            rows, w = slice(tb * HD, (tb + 1) * HD), (tb + 1) * HD
            mask = causal(tb)[:, 0:w]
            lc = lcol[rows]
            ds = jnp.zeros((HD, w), F32)
            sums = jnp.zeros((HD, HD), F32)
            for h in range(HEADS):
                dm = mm_nt(mixg[rows, hc(h)], xd[0:w, hc(h)])
                e = jnp.exp(jnp.where(mask, lc[:, h : h + 1] - lrow[h : h + 1, 0:w], -1e30))
                ds = ds + dm * e
                row_sum = jnp.sum(dm * pbuf[h, rows, 0:w].astype(F32), axis=-1, keepdims=True)
                sums = jnp.where(small_lane == h, row_sum, sums)
            dl[rows] = sums
            dsb = (ds * SCALE).astype(BF16)
            projg[rows, 640:768] = mm(dsb, proj[0:w, 512:640]).astype(BF16)
            contrib = mm_tn(dsb, proj[rows, 640:768])
            if tb:
                acc[0, 0 : w - HD] = acc[0, 0 : w - HD] + contrib[0 : w - HD]
            acc[0, w - HD : w] = contrib[w - HD :]

        projg[:, 512:640] = acc[0].astype(BF16)
        dt = dtb[...]
        dlv = dl[...]
        cpv = jnp.zeros((SEQ, HD), F32)
        for h in range(HEADS):
            dxp = jnp.concatenate(
                [mm_tn(pbuf[h, sb:, sb : sb + HD], mixg[sb:, hc(h)]) for sb in range(0, SEQ, HD)], axis=0
            )
            projg[:, hc(h)] = (dxp * dt[:, h : h + 1]).astype(BF16)
            col = jnp.sum(dxp * xd[:, hc(h)].astype(F32), axis=-1, keepdims=True)
            colp = jnp.sum(dxp * proj[:, hc(h)].astype(F32), axis=-1, keepdims=True)
            dlv = jnp.where(lane == h, dlv - col, dlv)
            cpv = jnp.where(lane == h, colp, cpv)
        triu = (
            lax.broadcasted_iota(jnp.int32, (SEQ, SEQ), 0) <= lax.broadcasted_iota(jnp.int32, (SEQ, SEQ), 1)
        ).astype(F32)
        rev = mm(triu, dlv, precision=HIGHEST)
        lgg = (cpv - rates_row() * rev) * jax.nn.sigmoid(lgb[...])
        lgg = jnp.where(lane < HEADS, lgg, 0.0)
        projg[:, 768:896] = lgg.astype(BF16)
        sm[d, :, 0:SEQ] = lgg.T[0:AUX, :].astype(BF16)
        rates = -jnp.sum(dt * rev, axis=0, keepdims=True)
        sm[d, :, SEQ:] = jnp.broadcast_to(rates, (AUX, HD)).astype(BF16)

    def attn_forward():
        @pl.loop(0, 4)
        def _(tb):
            rows = pl.ds(aligned(tb * HD, HD), HD)
            mask = causal(tb)
            for h in range(HEADS):
                s = jnp.where(mask, mm_nt(proj[rows, hc(h)], proj[:, 512:640]) * SCALE, -1e30)
                e = jnp.exp(s - jnp.max(s, axis=-1, keepdims=True))
                w = (e / jnp.sum(e, axis=-1, keepdims=True)).astype(BF16)
                pbuf[h, rows] = w
                mixed[rows, hc(h)] = mm(w, proj[:, 640:768]).astype(BF16)

    def attn_backward():
        for tb in range(4):
            rows, w = slice(tb * HD, (tb + 1) * HD), (tb + 1) * HD
            ds_all, q_all, w_all, g_all = [], [], [], []
            for h in range(HEADS):
                gb = mixg[rows, hc(h)]
                wb = pbuf[h, rows, 0:w]
                ww = wb.astype(F32)
                dw = mm_nt(gb, proj[0:w, 640:768])
                ds = (ww * (dw - jnp.sum(ww * dw, axis=-1, keepdims=True)) * SCALE).astype(BF16)
                projg[rows, hc(h)] = mm(ds, proj[0:w, 512:640]).astype(BF16)
                ds_all.append(ds)
                w_all.append(wb)
                g_all.append(gb)
                q_all.append(proj[rows, hc(h)])
            dk = mm_tn(jnp.concatenate(ds_all, axis=0), jnp.concatenate(q_all, axis=0))
            dv = mm_tn(jnp.concatenate(w_all, axis=0), jnp.concatenate(g_all, axis=0))
            if tb:
                acc[0, 0 : w - HD] = acc[0, 0 : w - HD] + dk[0 : w - HD]
                acc[1, 0 : w - HD] = acc[1, 0 : w - HD] + dv[0 : w - HD]
            acc[0, w - HD : w] = dk[w - HD :]
            acc[1, w - HD : w] = dv[w - HD :]
        projg[:, 512:640] = acc[0].astype(BF16)
        projg[:, 640:768] = acc[1].astype(BF16)
        projg[:, 768:896] = jnp.zeros((SEQ, HD), BF16)

    def scatter_terms(after_chunk, beside):
        for h in range(CH):
            for cc in range(2):
                for xx in range(4):
                    src = (xx * 2 + cc) * OWN + h * HS
                    dst = (cc * 4 + xx) * HS
                    pgc[h, dst : dst + HS] = projg[src : src + HS]

        def rows_of(h, xx, half=None):
            rows = pl.ds(aligned(xx * HS, HS), HS)
            if half is None:
                return terms.at[h, c, rows]
            return terms.at[h, c, rows, pl.ds(half * HALF, HALF)]

        def copies(h):
            return dict(
                sib=rc(("x", h, "sib"), terms.at[h, 1 - c], xsib.at[h], sib),
                r1=rc(("x", h, "r1"), rows_of(h, x2, 0), rl.at[h, 0], right),
                l1=rc(("x", h, "l1"), rows_of(h, x2, 1), rl.at[h, 1], left),
                r2=rc(("x", h, "r2"), rows_of(h, xr, 1), rb.at[h, 0, :, pl.ds(HALF, HALF)], right),
                l2=rc(("x", h, "l2"), rows_of(h, xl, 0), rb.at[h, 1, :, pl.ds(0, HALF)], left),
                r3=rc(("x", h, "r3"), rows_of(h, xr, 0), rb.at[h, 0, :, pl.ds(0, HALF)], right),
                l3=rc(("x", h, "l3"), rows_of(h, xl, 1), rb.at[h, 1, :, pl.ds(HALF, HALF)], left),
            )

        cs = [copies(h) for h in range(CH)]

        def stage_a(h):
            lhs = pgc[h : h + 2].reshape(16 * HS, BW + HD)

            @pl.loop(0, 4)
            def _(n):
                cols = pl.ds(aligned(n * 1024, 1024), 1024)
                val = mm_nt(lhs[:, 0:BW], inw[cols, :]) + mm(lhs[:, BW : BW + AUX], swt_ref[:, cols])
                val = val.astype(BF16)
                for i in range(4):
                    terms[h + i // 2, i % 2, :, cols] = val[i * 64 : (i + 1) * 64]

            cs[h]["sib"].start()
            cs[h + 1]["sib"].start()

        def stage_b(h):
            cs[h]["sib"].wait_recv()

            @pl.loop(0, 4)
            def _(i):
                rows = pl.ds(aligned(i * HS, HS), HS)
                terms[h, c, rows] = (terms[h, c, rows].astype(F32) + xsib[h, rows].astype(F32)).astype(BF16)

            cs[h]["r1"].start()
            cs[h]["l1"].start()

        def stage_e(h):
            cs[h]["r2"].start()
            cs[h]["l2"].start()

        def stage_c(h):
            cs[h]["r1"].wait_recv()
            rows, cols = pl.ds(aligned(xr * HS, HS), HS), pl.ds(0, HALF)
            terms[h, c, rows, cols] = (terms[h, c, rows, cols].astype(F32) + rl[h, 0].astype(F32)).astype(BF16)
            cs[h]["r3"].start()
            cs[h]["l1"].wait_recv()
            rows, cols = pl.ds(aligned(xl * HS, HS), HS), pl.ds(HALF, HALF)
            terms[h, c, rows, cols] = (terms[h, c, rows, cols].astype(F32) + rl[h, 1].astype(F32)).astype(BF16)
            cs[h]["l3"].start()

        def stage_d(h):
            for k in ("r2", "l2", "r3", "l3"):
                cs[h][k].wait_recv()
            rows = pl.ds(aligned(x * HS, HS), HS)
            ng = terms[h, c, rows].astype(F32) + rb[h, 0].astype(F32) + rb[h, 1].astype(F32)
            mine = slice(h * HS, (h + 1) * HS)
            xv = x_ref[mine].astype(F32)
            r = lax.rsqrt(jnp.mean(xv * xv, axis=-1, keepdims=True) + 1e-05)
            term = jnp.sum(xv * r * ng, axis=0, keepdims=True)
            for i in range(8):
                part = term[:, i * 512 : (i + 1) * 512]
                gacc[0, i : i + 1] = part if h == 0 else gacc[0, i : i + 1] + part
            ngg = ng * gain_ref[...].astype(F32)
            dot = jnp.mean(xv * ngg, axis=-1, keepdims=True)
            dy = up[pl.ds(base(x, c, h * HS), HS)].astype(F32)
            ig_ref[mine] = (dy + r * ngg - xv * (r * r * r * dot)).astype(BF16)
            after_chunk(h)

        plan = ("a0", "b0", "e0", "b1", "a2", "c0", "e1", "b2", "c1", "d0", "e2", "b3", "c2", "d1", "e3", "c3", "d2", "d3")
        stages = dict(a=stage_a, b=stage_b, c=stage_c, d=stage_d, e=stage_e)
        for i, step in enumerate(plan):
            stages[step[0]](int(step[1]))
            for extra in beside.get(step, ()):
                extra()
        for h in range(CH):
            for k in cs[h]:
                cs[h][k].wait_send()

    def handed(h):
        rows = pl.ds(base(x, c, h * HS), HS)
        return rc(("z", h), ig_ref.at[pl.ds(h * HS, HS)], up.at[rows], other)

    class Spread:
        def __init__(self, key, buf):
            first, rest = pl.ds(0, NA), pl.ds(NA, SEQ - NA)
            hb = (SEQ - NA) // 2
            low, high = pl.ds(NA, hb), pl.ds(NA + hb, hb)
            self.all = []

            def move(name, yy, zz, rows, dev):
                ref = buf.at[yy * 2 + zz, rows]
                copy = rc((key, name), ref, ref, dev)
                self.all.append(copy)
                return copy

            self.za = move("za", y, z, first, zpar)
            self.ua, self.da = move("ua", y, z, first, upper), move("da", y, z, first, lower)
            self.up, self.dp = move("up", y, 1 - z, first, upper), move("dp", y, 1 - z, first, lower)
            self.ur, self.dr = move("ur", yd, z, first, upper), move("dr", yu, 1 - z, first, lower)
            self.ub, self.db = move("ub", y, z, rest, upper), move("db", y, z, rest, lower)
            self.ubr, self.dbr = move("ubr", yd, z, low, upper), move("dbr", yu, z, high, lower)
            self.zb = [move(("zb", k), yy, z, rest, zpar) for k, yy in enumerate((y, yd, yu, y2))]

        def start(self):
            for copy in (self.za, self.ub, self.db, self.ua, self.da, self.zb[0]):
                copy.start()

        def s1(self):
            self.ub.wait_recv()
            self.ubr.start()
            self.zb[1].start()
            self.db.wait_recv()
            self.dbr.start()
            self.zb[2].start()

        def s2(self):
            self.za.wait_recv()
            self.up.start()
            self.dp.start()

        def s3(self):
            self.ubr.wait_recv()
            self.dbr.wait_recv()
            self.zb[3].start()

        def s4(self):
            self.ua.wait_recv()
            self.ur.start()

        def s5(self):
            self.da.wait_recv()
            self.up.wait_recv()
            self.dp.wait_recv()
            self.dr.start()

        def end(self, use=lambda yy, zz: None):
            self.zb[0].wait_recv()
            use(y, 1 - z)
            self.zb[1].wait_recv()
            use(yd, 1 - z)
            self.zb[2].wait_recv()
            use(yu, 1 - z)
            self.ur.wait_recv()
            use(y2, z)
            self.zb[3].wait_recv()
            self.dr.wait_recv()
            use(y2, 1 - z)

        def sent(self):
            for copy in self.all:
                copy.wait_send()

    mix_all, grad_all = Spread("m", ma), Spread("p", pa)

    def mix_start():
        ma[d] = mixed[...]
        mix_all.start()

    def grad_start():
        pa[d] = projg[:, 0:BW]
        grad_all.start()

    def out_sum():
        outg_ref[...] = mm_tn(ma[0], dd[0])

        @pl.loop(1, 8)
        def _(r):
            outg_ref[...] = outg_ref[...] + mm_tn(ma[r], dd[r])

    def in_first():
        ing_ref[...] = mm_tn(nd[d], pa[d])

    def in_add(yy, zz):
        k = yy * 2 + zz
        ing_ref[...] = ing_ref[...] + mm_tn(nd[k], pa[k])

    sms = [rc(("sm", rel), sm.at[d], sm.at[d], dev) for rel, dev in peers.items()]
    rec = rc("rec", aux_ref, auxr, other)

    def small_start():
        for copy in sms:
            copy.start()

    def small_end():
        for copy in sms:
            copy.wait_recv()
        steps = jnp.zeros((AUX, 512), F32)
        rates = jnp.zeros((AUX, HD), F32)
        for r in range(8):
            steps = steps + mm(sm[r, :, 0:SEQ], nd[r])
            rates = rates + sm[r, :, SEQ:].astype(F32)
        aux_ref[...] = jnp.zeros_like(aux_ref)
        aux_ref[:, 0:512] = steps
        aux_ref[:, 512:640] = rates
        rec.start()

    def gmove(name, a, b, dev):
        return rc(("gain", name), gacc.at[a], gx.at[b], dev)

    g_core = [gmove("c", 0, 0, sib)]
    g_x = [gmove("x0", 1, 1, right), gmove("x1", 1, 2, left), gmove("x2", 1, 3, far)]
    g_y = [gmove("y0", 2, 4, upper), gmove("y1", 2, 5, lower), gmove("y2", 2, 6, yfar)]
    g_z = [gmove("z", 3, 7, zpar)]

    def gain_start(group):
        for copy in group:
            copy.start()

    def gain_add(group, at, slots):
        for copy in group:
            copy.wait_recv()
        total = gacc[at]
        for k in slots:
            total = total + gx[k]
        gacc[at + 1] = total

    def gain_1():
        gain_start(g_core)

    def gain_2():
        gain_add(g_core, 0, (0,))
        gain_start(g_x)

    def gain_3():
        gain_add(g_x, 1, (1, 2, 3))
        gain_start(g_y)

    def gain_4():
        gain_add(g_y, 2, (4, 5, 6))
        gain_start(g_z)

    def gain_5():
        gain_add(g_z, 3, (7,))
        whole = gacc[4]
        mine = jnp.where(lax.broadcasted_iota(jnp.int32, (8, 512), 0) == d, whole, 0.0)
        pick = (
            lax.broadcasted_iota(jnp.int32, (512, 64), 0) == lax.broadcasted_iota(jnp.int32, (512, 64), 1) + t * 64
        ).astype(F32)
        gaing_ref[...] = jnp.sum(mm(mine, pick, precision=HIGHEST), axis=0, keepdims=True)
        for copy in g_core + g_x + g_y + g_z:
            copy.wait_send()

    @pl.when(p == 1)
    def _():
        ssm_steps()
        _st, u_mid, u_end, u_sent = gather("u", up, 0, OWN)
        u_mid()
        ssm_forward()
        ns_arrive()
        nx_start()
        mix_start()
        u_end()
        cp_out.wait()
        mix_gradient()
        ssm_backward()
        nx_mid()
        small_start()
        scatter_terms(lambda h: handed(h).start(), {})
        grad_start()
        nx_end()
        gain_1()
        ds_arrive()
        dx_start()
        mix_all.s1()
        mix_all.s2()
        gain_2()
        grad_all.s1()
        mix_all.s3()
        gain_3()
        mix_all.s4()
        mix_all.s5()
        grad_all.s2()
        dx_mid()
        gain_4()
        grad_all.s3()
        grad_all.s4()
        grad_all.s5()
        gain_5()
        dx_end()
        small_end()
        mix_all.end()
        out_sum()
        in_first()
        in_add(yu, z)
        in_add(yd, z)
        grad_all.end(in_add)
        u_sent()
        for h in range(CH):
            handed(h).wait_send()
        for copy in sms:
            copy.wait_send()
        rec.wait_send()

    @pl.when(p == 0)
    def _():
        attn_forward()
        ns_arrive()
        nx_start()
        mix_start()
        mix_all.s1()
        mix_all.s2()
        nx_mid()
        mix_all.s3()
        mix_all.s4()
        mix_all.s5()
        nx_end()
        gs = [gather(("e", h), up, h * HS, HS) for h in range(CH)]

        def arrive(h):
            handed(h).wait_recv()
            gs[h][0]()

        arrive(0)
        for h in range(1, CH):
            arrive(h)
            gs[h - 1][1]()
            if h >= 2:
                gs[h - 2][2]()
        ds_start()
        gs[CH - 1][1]()
        gs[CH - 2][2]()
        gs[CH - 1][2]()
        cp_out.wait()
        mix_gradient()
        ds_arrive()
        dx_start()
        attn_backward()
        grad_start()
        in_first()
        mix_all.end()
        scatter_terms(
            lambda h: None,
            {
                "a0": [dx_mid],
                "b1": [grad_all.s1, grad_all.s2],
                "a2": [dx_end],
                "c1": [out_sum],
                "d0": [grad_all.s3],
                "d1": [grad_all.s4],
            },
        )
        gain_1()
        grad_all.s5()
        gain_2()
        in_add(yu, z)
        gain_3()
        in_add(yd, z)
        gain_4()
        gain_5()
        grad_all.end(in_add)
        for h in range(CH):
            gs[h][3]()
        rec.wait_recv()
        aux_ref[...] = auxr[...]

    n_sent()
    ns_sent()
    ds_sent()
    nx_sent()
    dx_sent()
    mix_all.sent()
    grad_all.sent()


NA = 288

N_SEMS = 240


def finish(ig_in, ing_in, outg_in, gaing_in, aux_in, ig, ing, outg, gaing, step, rates, b0, b1, b2, sems):
    ins, outs = [], []
    for src, mid, dst in ((ing_in, b1, ing), (outg_in, b2, outg), (ig_in, b0, ig)):
        n = src.shape[0] // 4
        for i in range(4):
            rows, k = pl.ds(i * n, n), len(ins)
            ins.append(pltpu.make_async_copy(src.at[rows], mid.at[rows], sems.at[0, k]))
            outs.append(pltpu.make_async_copy(mid.at[rows], dst.at[rows], sems.at[1, k]))
    for copy in ins:
        copy.start()
    for k in range(len(ins)):
        ins[k].wait()
        outs[k].start()
    gaing[...] = gaing_in[...]
    p = lax.axis_index("pipe")
    rows = jnp.where(p == 0, aux_in[:, 0:256], aux_in[:, 256:512])
    step[...] = rows[0:HEADS]
    rates[...] = aux_in[0:1, 512 : 512 + HEADS]
    for copy in outs:
        copy.wait()


def shards(section_inputs, grad_out, in_weight, out_weight, gains, step_weight, decay_rate):
    vm = pl.BlockSpec(memory_space=pltpu.VMEM)
    hbm = pl.BlockSpec(memory_space=pl.ANY)
    v = pltpu.VMEM
    far = pl.BlockSpec(memory_space=pltpu.HBM)
    ig, ing, outg, gaing, aux = pl.pallas_call(
        kernel,
        out_shape=(
            jax.ShapeDtypeStruct((OWN, D), BF16),
            jax.ShapeDtypeStruct((512, BW), F32),
            jax.ShapeDtypeStruct((MW, 512), F32),
            jax.ShapeDtypeStruct((1, 64), F32),
            jax.ShapeDtypeStruct((AUX, BW), F32),
        ),
        in_specs=[vm, hbm, hbm, hbm, vm, vm, pl.BlockSpec(memory_space=pltpu.SMEM)],
        out_specs=(vm, vm, vm, vm, vm),
        scratch_shapes=[
            v((SEQ, D), BF16),
            v((SEQ, D), BF16),
            v((D, BW), BF16),
            v((MW, D), BF16),
            v((SEQ, BW), BF16),
            v((SEQ, BW + HD), BF16),
            v((SEQ, MW), BF16),
            v((SEQ, MW), BF16),
            v((HEADS, SEQ, SEQ), BF16),
            v((SEQ, MW), BF16),
            v((HD, SEQ), F32),
            v((SEQ, HD), F32),
            v((SEQ, HD), F32),
            v((SEQ, HD), F32),
            v((SEQ, HD), F32),
            v((2, SEQ, HD), F32),
            v((CH, 8 * HS, BW + HD), BF16),
            v((CH, 2, 4 * HS, D), BF16),
            v((CH, 4 * HS, D), BF16),
            v((CH, 2, HS, HALF), BF16),
            v((CH, 2, HS, D), BF16),
            v((8, SEQ, 512), BF16),
            v((8, SEQ, 512), BF16),
            v((8, SEQ, MW), BF16),
            v((8, SEQ, BW), BF16),
            v((8, AUX, SEQ + HD), BF16),
            v((5, 8, 512), F32),
            v((8, 8, 512), F32),
            v((AUX, BW), F32),
            v((AUX, D), BF16),
            pltpu.SemaphoreType.DMA((3,)),
            pltpu.SemaphoreType.DMA((N_SEMS,)),
            pltpu.SemaphoreType.DMA((N_SEMS,)),
        ],
        compiler_params=pltpu.CompilerParams(
            collective_id=0, has_side_effects=True, vmem_limit_bytes=63 << 20
        ),
    )(
        section_inputs[0, 0, 0], grad_out[0, 0], in_weight[0], out_weight[0], gains, step_weight.T, decay_rate
    )
    ig, ing, outg, gaing, step, rates = pl.pallas_call(
        finish,
        out_shape=(
            jax.ShapeDtypeStruct((OWN, D), BF16),
            jax.ShapeDtypeStruct((512, BW), F32),
            jax.ShapeDtypeStruct((MW, 512), F32),
            jax.ShapeDtypeStruct((1, 64), F32),
            jax.ShapeDtypeStruct((HEADS, 256), F32),
            jax.ShapeDtypeStruct((1, HEADS), F32),
        ),
        in_specs=[far, far, far, vm, vm],
        out_specs=(far, far, far, vm, vm, vm),
        scratch_shapes=[
            v((OWN, D), BF16),
            v((512, BW), F32),
            v((MW, 512), F32),
            pltpu.SemaphoreType.DMA((2, 12)),
        ],
        compiler_params=pltpu.CompilerParams(vmem_limit_bytes=60 << 20),
    )(ig, ing, outg, gaing, aux)
    return (ig[None, None, None], ing[None], outg[None], gaing, step.T, rates[0])


def solution(mesh):
    return jax.shard_map(
        shards,
        mesh=mesh,
        in_specs=(
            P("dp", "pipe", None, "ts", None),
            P("dp", None, "ts", None),
            P("pipe", None, "ts"),
            P("pipe", "ts", None),
            P("pipe", None),
            P(None, "ts"),
            P("ts"),
        ),
        out_specs=(
            P("dp", "pipe", None, "ts", None),
            P("pipe", "dp", "ts"),
            P("pipe", "ts", "dp"),
            P("pipe", ("dp", "ts")),
            P(("dp", "pipe"), "ts"),
            P("ts"),
        ),
        check_vma=False,
    )
```

time: 856 us -> 166 us (0.19); the launches traced: 847 us -> 166 us
  blocking collectives: 367 us -> 0 us
  waiting for transfers between devices: 277 us -> 0 us
  Pallas kernels: 0 us -> 165 us
  matrix products: 82 us -> 0 us
  local copies, waits for them, and re-layouts: 59.9 us -> 0 us
  other arithmetic: 29.8 us -> 0 us
  loops' own time: 14.7 us -> 0 us
  between operations: 15.2 us -> 0.82 us
    unnamed x1 -> x0, blocking collectives: 330 us -> none
    pallas_call x0 -> x2, Pallas kernels: none -> 165 us  [the longest x1 161 us: shards(): pl.pallas_call(kernel, out_shape=(jax.ShapeDtypeStruct((OWN, D), BF16), j...]
    reduce_scatter x3 -> x0, waiting for transfers between devices: 157 us -> none  [the longest x2 157 us: shards(): lax.psum_scatter(terms.astype(jnp.bfloat16), 'ts', scatter_dimension=0, t...]
    all_gather x3 -> x0, waiting for transfers between devices: 94.4 us -> none  [the longest x2 60 us: shards(): lax.all_gather(incoming, 'ts', axis=0, tiled=True)]
    dot_general x15 -> x0, matrix products: 82 us -> none  [the longest x3 19.1 us: attend(): jnp.einsum('hst,td->shd', weights, values_part, precision=highest)]
    another operation x44 -> x0, local copies, waits for them, and re-layouts: 45.7 us -> none
    psum x1 -> x0, blocking collectives: 36.6 us -> none  [shards(): rate_out = lax.psum(rate_acc, ('dp', 'pipe'))]
    unnamed x8 -> x0, waiting for transfers between devices: 13.7 us -> none
  transfers between devices with their start and end apart: 8 -> 0, of which waited for: 7 -> 0; matrix products, arithmetic and copies ran while one was open for 4% -> 0% of each run, Pallas kernels for 0% -> 0%
where the time goes in v1:
time: 166 us
  Pallas kernels  165 us (99%)
    pallas_call x1, Pallas kernels, shards(): pl.pallas_call(kernel, out_shape=(jax.ShapeDtypeStruct((OWN, D), BF16), j...  161 us
    pallas_call x1, Pallas kernels, shards(): pl.pallas_call(finish, out_shape=(jax.ShapeDtypeStruct((OWN, D), BF16), j...  4.25 us

profile of v1, /device:TPU:0, one launch (start us, length us, event | category | flops | bytes accessed | tf_op | source)
XLA Modules:
  0.0 165.9 jit_solution(15713082925688516827)
XLA Ops:
  0.6 160.8 %shard_map.118 = (bf16[64,4096]{1,0:T(8,128)(2,1)}, f32[512,768]{1,0:T(8,128)}, f32[512,512]{1,0:T(8,128)}, f32[1,64]{1,0:T(1,128)}, f32[16,768]{1,0:T(8,128)}) custom-call(bf16[64,4096]{1,0:T(8,128)(2,1)} %bitcast.12, bf16[64,4096]{1,0:T(8,128)(2,1)} %bitcast.13, bf16[4096,768]{1,0:T(8,128)(2,1)} %bitcast.10, bf16[512,4096]{1,0:T(8,128)(2,1)} %bitcast.11, ...), custom_call_target="tpu_custom_call" | custom-call | tf_op jit(solution)/shard_map/pallas_call | solution.py:737
  161.5 4.2 %shard_map.119 = (bf16[64,4096]{1,0:T(8,128)(2,1)}, f32[512,768]{1,0:T(8,128)}, f32[512,512]{1,0:T(8,128)}, f32[1,64]{1,0:T(1,128)}, f32[4,256]{1,0:T(4,128)}, /*index=5*/f32[1,4]{1,0:T(1,128)}) custom-call(bf16[64,4096]{1,0:T(8,128)(2,1)} %get-tuple-element.17.ig_in, f32[512,768]{1,0:T(8,128)} %get-tuple-element.18.ing_in, ...), custom_call_target="tpu_custom_call" | custom-call | tf_op jit(solution)/shard_map/pallas_call | solution.py:789
